TPU v7x, 32 devices: a whole 2x2x4 slice. The times are simulated.
32 devices in a mesh: gx: 4 (over y, core), gy: 8 (over z, x).
Axes of the slice: x: 2, y: 2, z: 4, core: 2. Of those that a mesh axis runs over, the one named last changes fastest.
Arguments:
- velocity: float32 [3, 32, 64, 512], P(None, 'gx', 'gy'), may hold values from -6 to 6
- stress: float32 [6, 32, 64, 512], P(None, 'gx', 'gy'), may hold values from -6 to 6
- lame_lambda: float32 [32, 64, 512], P('gx', 'gy'), may hold values from 0.5 to 5
- lame_mu: float32 [32, 64, 512], P('gx', 'gy'), may hold values from 0.5 to 5
- node_mass: float32 [32, 64, 512], P('gx', 'gy'), may hold values from 0.5 to 2
- displacement: float32 [3, 32, 64, 512], P(None, 'gx', 'gy'), may hold values from -0.75 to 0.75
- seg_elem: int32 [65536], P(('gx', 'gy')), may hold values from 0 to 32767
- seg_bucket: int32 [65536, 1], P(('gx', 'gy')), may hold values from 0 to 31; in each aligned block of 2048 rows (0 to 2047, 2048 to 4095, ...) at most 128 rows name the same one
- slave_points: float32 [3, 16384], P(None, ('gx', 'gy')), may hold values from 0.8 to 1.2
- candidates: int32 [4, 16384], P(None, ('gx', 'gy')), may hold values from 0 to 4095
Outputs:
- new_stress: float32 [6, 32, 64, 512], P(None, 'gx', 'gy')
- acceleration: float32 [3, 32, 64, 512], P(None, 'gx', 'gy')
- slave_force: float32 [3, 16384], P(None, ('gx', 'gy'))
Inputs may be any that keep to these rules, and one draw needn't show every extreme that they name: `seg_bucket`: in the rows of one device no bucket is named more than 128 times. `candidates`: A slot index into the 32 x 128 segment slots of the slave's own bucket, source device major; a slot holding no segment contributes nothing.
All inputs are finite; a program needn't handle non-finite values.
Results may differ from a plain program's by a relative error of at most 0.0003.
Values sent between devices are 32-bit elements; how exact they have to be, the bound alone decides.
A program may use at most 128 MiB of HBM per device.

v0:
```python
import jax
import jax.numpy as jnp
from jax import lax
from jax.sharding import PartitionSpec as P

time_step = 0.1
penalty = 10.0


def shifted(array, axis, by):
    size = lax.axis_size(axis)
    pairs = [(i, i + by) for i in range(size) if 0 <= i + by < size]
    return lax.ppermute(array, axis, pairs)


def element_pass(extended, stress, lame_lambda, lame_mu):
    size_x = extended.shape[1] - 1
    size_y = extended.shape[2] - 1
    size_z = extended.shape[3] - 1
    nodal = extended[0:3]

    def corner_vel(side_x, side_y, side_z):
        return nodal[
            :, side_x : side_x + size_x, side_y : side_y + size_y, side_z : side_z + size_z
        ]

    grad_x = 0.25 * sum((corner_vel(1, p, q) - corner_vel(0, p, q) for p in (0, 1) for q in (0, 1)))
    grad_y = 0.25 * sum((corner_vel(p, 1, q) - corner_vel(p, 0, q) for p in (0, 1) for q in (0, 1)))
    grad_z = 0.25 * sum((corner_vel(p, q, 1) - corner_vel(p, q, 0) for p in (0, 1) for q in (0, 1)))
    rate_xx = grad_x[0]
    rate_yy = grad_y[1]
    rate_zz = grad_z[2]
    rate_yz = 0.5 * (grad_z[1] + grad_y[2])
    rate_xz = 0.5 * (grad_z[0] + grad_x[2])
    rate_xy = 0.5 * (grad_y[0] + grad_x[1])
    volume_rate = rate_xx + rate_yy + rate_zz
    stress_xx = stress[0] + time_step * (lame_lambda * volume_rate + 2.0 * lame_mu * rate_xx)
    stress_yy = stress[1] + time_step * (lame_lambda * volume_rate + 2.0 * lame_mu * rate_yy)
    stress_zz = stress[2] + time_step * (lame_lambda * volume_rate + 2.0 * lame_mu * rate_zz)
    stress_yz = stress[3] + time_step * 2.0 * lame_mu * rate_yz
    stress_xz = stress[4] + time_step * 2.0 * lame_mu * rate_xz
    stress_xy = stress[5] + time_step * 2.0 * lame_mu * rate_xy
    new_stress = jnp.stack([stress_xx, stress_yy, stress_zz, stress_yz, stress_xz, stress_xy])
    tensor = (
        (stress_xx, stress_xy, stress_xz),
        (stress_xy, stress_yy, stress_yz),
        (stress_xz, stress_yz, stress_zz),
    )
    forces = jnp.zeros((3, size_x + 1, size_y + 1, size_z + 1), extended.dtype)
    for side_x in (0, 1):
        for side_y in (0, 1):
            for side_z in (0, 1):
                sign_x = 2.0 * side_x - 1.0
                sign_y = 2.0 * side_y - 1.0
                sign_z = 2.0 * side_z - 1.0
                part = jnp.stack(
                    [
                        -0.25
                        * (
                            sign_x * tensor[row][0]
                            + sign_y * tensor[row][1]
                            + sign_z * tensor[row][2]
                        )
                        for row in range(3)
                    ]
                )
                forces = forces + jnp.pad(
                    part, ((0, 0), (side_x, 1 - side_x), (side_y, 1 - side_y), (side_z, 1 - side_z))
                )
    return (new_stress, forces)


def seg_geometry(corners):
    low_low = corners[0:3]
    high_low = corners[3:6]
    high_high = corners[6:9]
    low_high = corners[9:12]
    centre = 0.25 * (low_low + high_low + high_high + low_high)
    first = high_high - low_low
    second = low_high - high_low
    area = 0.5 * jnp.stack(
        [
            first[1] * second[2] - first[2] * second[1],
            first[2] * second[0] - first[0] * second[2],
            first[0] * second[1] - first[1] * second[0],
        ]
    )
    return (centre, area)


def slot_rank(bucket, devices):
    onehot = (bucket[:, None] == jnp.arange(devices, dtype=jnp.int32)[None, :]).astype(jnp.int32)
    running = jnp.cumsum(onehot, axis=0)
    return jnp.sum(running * onehot, axis=1) - 1


def per_device(
    velocity,
    stress,
    lame_lambda,
    lame_mu,
    node_mass,
    displacement,
    seg_elem,
    seg_bucket,
    slave_points,
    candidates,
):
    count_x = lax.axis_size("gx")
    count_y = lax.axis_size("gy")
    devices = count_x * count_y
    size_x = velocity.shape[1]
    size_y = velocity.shape[2]
    size_z = velocity.shape[3]
    seg_count = seg_elem.shape[0]
    capacity = 2 * seg_count // devices
    slots = devices * capacity
    own = jnp.concatenate([velocity, displacement], 0)
    ghost_x = shifted(own[:, :1], "gx", -1)
    extended = jnp.concatenate([own, ghost_x], 1)
    ghost_y = shifted(extended[:, :, :1], "gy", -1)
    extended = jnp.concatenate([extended, ghost_y], 2)
    extended = jnp.pad(extended, ((0, 0), (0, 0), (0, 0), (0, 1)))
    new_stress, forces = element_pass(extended, stress, lame_lambda, lame_mu)
    bucket = seg_bucket[:, 0]
    ranks = slot_rank(bucket, devices)
    target = bucket * capacity + ranks
    cell_i = seg_elem // (size_y * size_z)
    cell_j = seg_elem // size_z % size_y
    cell_k = seg_elem % size_z
    flat_disp = extended[3:6].reshape(3, -1)
    offsets = ((0, 0), (1, 0), (1, 1), (0, 1))
    indices = []
    pieces = []
    for off_a, off_b in offsets:
        index = ((cell_i + off_a) * (size_y + 1) + cell_j + off_b) * (size_z + 1) + cell_k + 1
        indices.append(index)
        shift_vec = jnp.array([off_a, off_b, 1.0], jnp.float32)[:, None]
        pieces.append(flat_disp[:, index] + shift_vec)
    corners = jnp.concatenate(pieces, 0)
    centre_own, area_own = seg_geometry(corners)
    payload = jnp.concatenate([centre_own, area_own], 0)
    width = payload.shape[0]
    outgoing = jnp.zeros((width, slots), jnp.float32).at[:, target].set(payload)
    arrived = lax.all_to_all(
        outgoing.reshape(width, devices, capacity),
        ("gx", "gy"),
        split_axis=1,
        concat_axis=1,
        tiled=True,
    )
    arrived = arrived.reshape(width, slots)
    centre = arrived[0:3]
    area = arrived[3:6]
    flat_candidates = candidates.reshape(-1)
    table = jnp.concatenate([centre, area], 0)
    near = table[:, flat_candidates].reshape(6, candidates.shape[0], candidates.shape[1])
    near_centre = near[0:3]
    near_area = near[3:6]
    gap = jnp.sum(near_area * (slave_points[:, None, :] - near_centre), axis=0)
    push = penalty * jnp.maximum(-gap, 0.0)[None] * near_area
    slave_force = jnp.sum(push, axis=1)
    reaction = jnp.zeros((3, slots), jnp.float32).at[:, flat_candidates].add(-push.reshape(3, -1))
    returned = lax.all_to_all(
        reaction.reshape(3, devices, capacity),
        ("gx", "gy"),
        split_axis=1,
        concat_axis=1,
        tiled=True,
    )
    returned = returned.reshape(3, slots)
    quarter = 0.25 * returned[:, target]
    flat_forces = forces.reshape(3, -1)
    for index in indices:
        flat_forces = flat_forces.at[:, index].add(quarter)
    forces = flat_forces.reshape(forces.shape)[:, :, :, :size_z]
    upper_y = shifted(forces[:, :, size_y : size_y + 1], "gy", 1)
    forces = forces[:, :, :size_y] + jnp.pad(upper_y, ((0, 0), (0, 0), (0, size_y - 1), (0, 0)))
    upper_x = shifted(forces[:, size_x : size_x + 1], "gx", 1)
    forces = forces[:, :size_x] + jnp.pad(upper_x, ((0, 0), (0, size_x - 1), (0, 0), (0, 0)))
    acceleration = forces / node_mass[None]
    return (new_stress, acceleration, slave_force)


def solution(mesh):
    return jax.shard_map(
        per_device,
        mesh=mesh,
        in_specs=(
            P(None, "gx", "gy", None),
            P(None, "gx", "gy", None),
            P("gx", "gy", None),
            P("gx", "gy", None),
            P("gx", "gy", None),
            P(None, "gx", "gy", None),
            P(("gx", "gy")),
            P(("gx", "gy"), None),
            P(None, ("gx", "gy")),
            P(None, ("gx", "gy")),
        ),
        out_specs=(P(None, "gx", "gy", None), P(None, "gx", "gy", None), P(None, ("gx", "gy"))),
        check_vma=False,
    )
```

profile of v0, /device:TPU:12, one launch (start us, length us, event | category | flops | bytes accessed | tf_op | source)
XLA Modules:
  0.0 286.3 jit_solution(2993142969272704066)
XLA Ops:
  4.8 9.1 %reduce-window.6 = s32[32,16,128]{2,1,0:T(8,128)S(1)} reduce-window(s32[32,16,128]{2,1,0:T(8,128)S(1)} %fusion.32, s32[]{:T(128)} %constant.89.clone.1), window={size=1x1x128 pad=0_0x0_0x127_0}, to_apply=%region_0.1 | reduce-window | flops 8323072 | bytes 524292 | tf_op jit(solution)/shard_map/reduce-window
  15.5 3.3 %collective-permute-start.1 = (f32[6,9,1,512]{3,2,1,0:T(1,128)S(1)}, f32[6,9,1,512]{3,2,1,0:T(1,128)S(1)}, u32[]{:S(2)}, u32[]{:S(2)}) collective-permute-start(f32[6,9,1,512]{3,2,1,0:T(1,128)S(1)} %pad_maximum_fusion.3), channel_id=1, source_target_pairs={{1,0},{2,1},{3,2},{4,3},{5,4},{6,5},{7,6},{9,8},{10,9},{11,10},{12... | collective-permute-start | bytes 331784 | tf_op jit(solution)/shard_map/ppermute | solution.py:13
  19.6 3.2 %collective-permute-done.1 = f32[6,9,1,512]{3,2,1,0:T(1,128)S(1)} collective-permute-done((f32[6,9,1,512]{3,2,1,0:T(1,128)S(1)}, f32[6,9,1,512]{3,2,1,0:T(1,128)S(1)}, u32[]{:S(2)}, u32[]{:S(2)}) %collective-permute-start.1) | collective-permute-done | bytes 110624 | tf_op jit(solution)/shard_map/ppermute | solution.py:13
  31.7 10.6 %copy.56 = f32[3,41553]{0,1:T(8,128)} copy(f32[3,41553]{1,0:T(4,128)S(1)} %reshape.123) | data formatting | bytes 997272 | tf_op jit(solution)/shard_map/reshape | solution.py:131
  42.3 12.5 %gather_fusion.3 = f32[2048,3]{1,0:T(8,128)S(1)} fusion(f32[3,41553]{0,1:T(8,128)} %copy.56, s32[2048]{0:T(1024)S(1)} %get-tuple-element.69), kind=kCustom, calls=%fused_computation.3 | custom fusion | bytes 57344 | tf_op jit(solution)/shard_map/gather | solution.py:139
  55.1 12.5 %gather_fusion.2 = f32[2048,3]{1,0:T(8,128)S(1)} fusion(f32[3,41553]{0,1:T(8,128)} %copy.56, s32[2048]{0:T(1024)S(1)} %get-tuple-element.67), kind=kCustom, calls=%fused_computation.2 | custom fusion | bytes 57344 | tf_op jit(solution)/shard_map/gather | solution.py:139
  68.1 12.5 %gather_fusion.1 = f32[2048,3]{1,0:T(8,128)S(1)} fusion(f32[3,41553]{0,1:T(8,128)} %copy.56, s32[2048]{0:T(1024)S(1)} %get-tuple-element.9), kind=kCustom, calls=%fused_computation.1 | custom fusion | bytes 57344 | tf_op jit(solution)/shard_map/gather | solution.py:139
  80.6 12.5 %gather_fusion = f32[2048,3]{1,0:T(8,128)S(1)} fusion(f32[3,41553]{0,1:T(8,128)} %copy.56, s32[2048]{0:T(1024)S(1)} %get-tuple-element.71), kind=kCustom, calls=%fused_computation | custom fusion | bytes 57344 | tf_op jit(solution)/shard_map/gather | solution.py:139
  94.4 6.2 %scatter_custom_fusion = f32[6,4096]{0,1:T(8,128)S(1)} fusion(s32[2048]{0:T(1024)} %bitcast.195, f32[2048,6]{1,0:T(8,128)S(1)} %copy.64, f32[]{:T(128)} %constant.80.clone.1), kind=kCustom, calls=%fused_computation.63 | custom fusion | bytes 98816 | tf_op jit(solution)/shard_map/scatter | solution.py:144
  102.0 5.9 %all-to-all-start = ((f32[6,32,128]{2,0,1:T(8,128)}), f32[6,32,128]{2,0,1:T(8,128)S(1)}, u32[]{:S(2)}, u32[]{:S(2)}) async-start(f32[6,32,128]{2,0,1:T(8,128)} %copy.65), calls=%async_computation | async-start | bytes 262144 | tf_op jit(solution)/shard_map/all_to_all | solution.py:145
  108.0 5.1 %fusion = f32[3,9,9,513]{3,2,1,0:T(8,128)} fusion(f32[1,8,8,512]{3,2,1,0:T(8,128)} %get-tuple-element.50, f32[1,8,8,512]{3,2,1,0:T(8,128)} %get-tuple-element.44, f32[1,8,8,512]{3,2,1,0:T(8,128)S(1)} %copy-done.9, f32[1,8,8,512]{3,2,1,0:T(8,128)} %get-tuple-element.49, f32[1,8,8,512]{3,2,1,0:T(8,128)} %get-tuple-element.43, ...), kind=kLoop, calls=%fused_computation.19 | loop fusion | flops 14086467 | bytes 3644364 | tf_op jit(solution)/shard_map/add | solution.py:67
  114.6 5.5 %gather_fusion.4 = f32[2048,6]{1,0:T(8,128)S(1)} fusion(f32[6,4096]{0,1:T(8,128)S(1)} %copy.66, s32[2048]{0:T(1024)S(1)} %get-tuple-element.73), kind=kCustom, calls=%fused_computation.4 | custom fusion | bytes 106496 | tf_op jit(solution)/shard_map/gather | solution.py:157
  122.4 13.1 %scatter_custom_fusion.1 = f32[3,4096]{0,1:T(8,128)S(1)} fusion(s32[2048]{0:T(1024)} %bitcast.199, f32[]{:T(128)} %constant.80.clone.1, f32[2048]{0:T(1024)S(1)} %maximum_multiply_fusion.1, f32[6,2048]{0,1:T(8,128)S(1)} %bitcast.184), kind=kCustom, calls=%fused_computation.58 | custom fusion | flops 18432 | bytes 107008 | tf_op jit(solution)/shard_map/scatter-add | solution.py:163
  136.8 5.6 %all-to-all-start.1 = ((f32[3,32,128]{2,0,1:T(4,128)}), f32[3,32,128]{2,0,1:T(4,128)S(1)}, u32[]{:S(2)}, u32[]{:S(2)}) async-start(f32[3,32,128]{2,0,1:T(4,128)} %copy.68), calls=%async_computation.1 | async-start | bytes 131072 | tf_op jit(solution)/shard_map/all_to_all | solution.py:164
  145.0 10.6 %copy.70 = f32[3,41553]{0,1:T(8,128)} copy(f32[3,41553]{1,0:T(4,128)S(1)} %reshape.120) | data formatting | bytes 997272 | tf_op jit(solution)/shard_map/reshape | solution.py:173
  156.3 5.5 %gather_fusion.5 = f32[2048,3]{1,0:T(8,128)S(1)} fusion(f32[3,4096]{0,1:T(8,128)S(1)} %bitcast.188, s32[2048]{0:T(1024)S(1)} %broadcast_clamp_fusion), kind=kCustom, calls=%fused_computation.5 | custom fusion | bytes 57344 | tf_op jit(solution)/shard_map/gather | solution.py:172
  161.8 24.6 %scatter_custom_fusion.2 = f32[3,41553]{0,1:T(8,128)} fusion(f32[3,41553]{0,1:T(8,128)} %copy.70, s32[2048]{0:T(1024)} %get-tuple-element.72, f32[2048,3]{1,0:T(8,128)S(1)} %gather_fusion.5, f32[]{:T(128)} %constant.81.clone.1), kind=kCustom, calls=%fused_computation.70 | custom fusion | flops 12288 | bytes 523724 | tf_op jit(solution)/shard_map/scatter-add | solution.py:175
  186.4 24.6 %scatter_custom_fusion.3 = f32[3,41553]{0,1:T(8,128)} fusion(f32[3,41553]{0,1:T(8,128)} %scatter_custom_fusion.2, s32[2048]{0:T(1024)} %get-tuple-element.10, f32[2048,3]{1,0:T(8,128)S(1)} %gather_fusion.5, f32[]{:T(128)} %constant.81.clone.1), kind=kCustom, calls=%fused_computation.68 | custom fusion | flops 12288 | bytes 523724 | tf_op jit(solution)/shard_map/scatter-add | solution.py:175
  211.0 24.6 %scatter_custom_fusion.4 = f32[3,41553]{0,1:T(8,128)} fusion(f32[3,41553]{0,1:T(8,128)} %scatter_custom_fusion.3, s32[2048]{0:T(1024)} %get-tuple-element.68, f32[2048,3]{1,0:T(8,128)S(1)} %gather_fusion.5, f32[]{:T(128)} %constant.81.clone.1), kind=kCustom, calls=%fused_computation.66 | custom fusion | flops 12288 | bytes 523724 | tf_op jit(solution)/shard_map/scatter-add | solution.py:175
  235.7 24.6 %scatter_custom_fusion.5 = f32[3,41553]{0,1:T(8,128)} fusion(f32[3,41553]{0,1:T(8,128)} %scatter_custom_fusion.4, s32[2048]{0:T(1024)} %get-tuple-element.70, f32[2048,3]{1,0:T(8,128)S(1)} %gather_fusion.5, f32[]{:T(128)} %constant.81.clone.1), kind=kCustom, calls=%fused_computation.72 | custom fusion | flops 12288 | bytes 523724 | tf_op jit(solution)/shard_map/scatter-add | solution.py:175
  260.3 12.0 %copy.71 = f32[3,41553]{1,0:T(4,128)S(1)} copy(f32[3,41553]{0,1:T(8,128)} %scatter_custom_fusion.5) | data formatting | bytes 997272 | tf_op jit(solution)/shard_map/scatter-add | solution.py:175
  272.9 3.5 %collective-permute-start.2 = (f32[3,9,1,512]{3,2,1,0:T(1,128)S(1)}, f32[3,9,1,512]{3,2,1,0:T(1,128)S(1)}, u32[]{:S(2)}, u32[]{:S(2)}) collective-permute-start(f32[3,9,1,512]{3,2,1,0:T(1,128)S(1)} %slice.256), channel_id=1, source_target_pairs={{0,1},{1,2},{2,3},{3,4},{4,5},{5,6},{6,7},{8,9},{9,10},{10,11},{11... | collective-permute-start | bytes 165896 | tf_op jit(solution)/shard_map/ppermute | solution.py:13
  277.1 2.9 %collective-permute-done.2 = f32[3,9,1,512]{3,2,1,0:T(1,128)S(1)} collective-permute-done((f32[3,9,1,512]{3,2,1,0:T(1,128)S(1)}, f32[3,9,1,512]{3,2,1,0:T(1,128)S(1)}, u32[]{:S(2)}, u32[]{:S(2)}) %collective-permute-start.2) | collective-permute-done | bytes 55328 | tf_op jit(solution)/shard_map/ppermute | solution.py:13
  283.1 2.4 collective-permute-done.3
  (112 shorter events, 32.0 us)
Async XLA Ops:
  0.6 4.0 %copy-start.19 = (s32[4,512]{1,0:T(4,128)S(1)}, s32[4,512]{1,0:T(4,128)}, u32[]{:S(2)}) copy-start(s32[4,512]{1,0:T(4,128)} %param.23) | copy-start | bytes 24580
  0.6 4.1 %copy-start.14 = (s32[2048,1]{0,1:T(1,128)S(1)}, s32[2048,1]{0,1:T(1,128)}, u32[]{:S(2)}) copy-start(s32[2048,1]{0,1:T(1,128)} %param.21) | copy-start | bytes 24580
  2.7 12.7 %collective-permute-start = (f32[6,1,8,512]{3,2,1,0:T(8,128)S(1)}, f32[6,1,8,512]{3,2,1,0:T(8,128)S(1)}, u32[]{:S(2)}, u32[]{:S(2)}) collective-permute-start(f32[6,1,8,512]{3,2,1,0:T(8,128)S(1)} %slice.231), channel_id=1, source_target_pairs={{8,0},{16,8},{24,16},{9,1},{17,9},{25,17},{10,2},{18,10},{26,18},{... | collective-permute-start | bytes 294920 | tf_op jit(solution)/shard_map/ppermute | solution.py:13
  4.7 10.0 %copy-start.16 = (s32[2048,1]{0,1:T(1,128)}, s32[2048,1]{0,1:T(1,128)S(1)}, u32[]{:S(2)}) copy-start(s32[2048,1]{0,1:T(1,128)S(1)} %compare_select_fusion.1) | copy-start | bytes 24580
  4.8 10.0 %copy-start.20 = (s32[2048]{0:T(1024)S(1)}, s32[2048]{0:T(1024)}, u32[]{:S(2)}) copy-start(s32[2048]{0:T(1024)} %param.20) | copy-start | bytes 24580
  14.0 4.8 %copy-start.18 = (f32[3,512]{1,0:T(4,128)S(1)}, f32[3,512]{1,0:T(4,128)}, u32[]{:S(2)}) copy-start(f32[3,512]{1,0:T(4,128)} %param.22) | copy-start | bytes 18436
  14.7 8.3 %copy-start.15 = (s32[2048,1]{0,1:T(1,128)}, s32[2048,1]{0,1:T(1,128)S(1)}, u32[]{:S(2)}) copy-start(s32[2048,1]{0,1:T(1,128)S(1)} %compare_select_fusion) | copy-start | bytes 24580
  15.5 7.4 %collective-permute-start.1 = (f32[6,9,1,512]{3,2,1,0:T(1,128)S(1)}, f32[6,9,1,512]{3,2,1,0:T(1,128)S(1)}, u32[]{:S(2)}, u32[]{:S(2)}) collective-permute-start(f32[6,9,1,512]{3,2,1,0:T(1,128)S(1)} %pad_maximum_fusion.3), channel_id=1, source_target_pairs={{1,0},{2,1},{3,2},{4,3},{5,4},{6,5},{7,6},{9,8},{10,9},{11,10},{12... | collective-permute-start | bytes 331784 | tf_op jit(solution)/shard_map/ppermute | solution.py:13
  26.4 2.0 copy-start.3
  31.7 10.6 %copy-start.17 = (f32[6,8,8,512]{3,2,1,0:T(8,128)}, f32[6,8,8,512]{3,2,1,0:T(8,128)S(1)}, u32[]{:S(2)}) copy-start(f32[6,8,8,512]{3,2,1,0:T(8,128)S(1)} %bitcast_dynamic-update-slice_fusion.3) | copy-start | bytes 2359300
  100.7 7.2 %copy-start.4 = (f32[1,8,8,512]{3,2,1,0:T(8,128)S(1)}, f32[1,8,8,512]{3,2,1,0:T(8,128)}, u32[]{:S(2)}) copy-start(f32[1,8,8,512]{3,2,1,0:T(8,128)} %get-tuple-element.17) | copy-start | bytes 393220
  100.7 7.2 %copy-start.5 = (f32[1,8,8,512]{3,2,1,0:T(8,128)S(1)}, f32[1,8,8,512]{3,2,1,0:T(8,128)}, u32[]{:S(2)}) copy-start(f32[1,8,8,512]{3,2,1,0:T(8,128)} %get-tuple-element.33) | copy-start | bytes 393220
  100.7 7.2 %copy-start.6 = (f32[1,8,8,512]{3,2,1,0:T(8,128)S(1)}, f32[1,8,8,512]{3,2,1,0:T(8,128)}, u32[]{:S(2)}) copy-start(f32[1,8,8,512]{3,2,1,0:T(8,128)} %get-tuple-element.34) | copy-start | bytes 393220
  100.7 7.2 %copy-start.7 = (f32[1,8,8,512]{3,2,1,0:T(8,128)S(1)}, f32[1,8,8,512]{3,2,1,0:T(8,128)}, u32[]{:S(2)}) copy-start(f32[1,8,8,512]{3,2,1,0:T(8,128)} %get-tuple-element.35) | copy-start | bytes 393220
  100.7 7.2 %copy-start.8 = (f32[1,8,8,512]{3,2,1,0:T(8,128)S(1)}, f32[1,8,8,512]{3,2,1,0:T(8,128)}, u32[]{:S(2)}) copy-start(f32[1,8,8,512]{3,2,1,0:T(8,128)} %get-tuple-element.36) | copy-start | bytes 393220
  100.7 7.2 %copy-start.9 = (f32[1,8,8,512]{3,2,1,0:T(8,128)S(1)}, f32[1,8,8,512]{3,2,1,0:T(8,128)}, u32[]{:S(2)}) copy-start(f32[1,8,8,512]{3,2,1,0:T(8,128)} %get-tuple-element.37) | copy-start | bytes 393220
  100.7 7.2 %copy-start.10 = (f32[1,8,8,512]{3,2,1,0:T(8,128)S(1)}, f32[1,8,8,512]{3,2,1,0:T(8,128)}, u32[]{:S(2)}) copy-start(f32[1,8,8,512]{3,2,1,0:T(8,128)} %get-tuple-element.38) | copy-start | bytes 393220
  100.7 7.2 %copy-start.11 = (f32[1,8,8,512]{3,2,1,0:T(8,128)S(1)}, f32[1,8,8,512]{3,2,1,0:T(8,128)}, u32[]{:S(2)}) copy-start(f32[1,8,8,512]{3,2,1,0:T(8,128)} %get-tuple-element.39) | copy-start | bytes 393220
  102.0 11.9 %all-to-all-start = ((f32[6,32,128]{2,0,1:T(8,128)}), f32[6,32,128]{2,0,1:T(8,128)S(1)}, u32[]{:S(2)}, u32[]{:S(2)}) async-start(f32[6,32,128]{2,0,1:T(8,128)} %copy.65), calls=%async_computation | async-start | bytes 262144 | tf_op jit(solution)/shard_map/all_to_all | solution.py:145
  136.8 18.9 %all-to-all-start.1 = ((f32[3,32,128]{2,0,1:T(4,128)}), f32[3,32,128]{2,0,1:T(4,128)S(1)}, u32[]{:S(2)}, u32[]{:S(2)}) async-start(f32[3,32,128]{2,0,1:T(4,128)} %copy.68), calls=%async_computation.1 | async-start | bytes 131072 | tf_op jit(solution)/shard_map/all_to_all | solution.py:164
  272.9 9.1 %copy-start = (f32[3,2048]{0,1:T(8,128)S(1)}, f32[3,2048]{0,1:T(8,128)}, u32[]{:S(2)}) copy-start(f32[3,2048]{0,1:T(8,128)} %get-tuple-element.31) | copy-start | bytes 73732
  272.9 7.1 %collective-permute-start.2 = (f32[3,9,1,512]{3,2,1,0:T(1,128)S(1)}, f32[3,9,1,512]{3,2,1,0:T(1,128)S(1)}, u32[]{:S(2)}, u32[]{:S(2)}) collective-permute-start(f32[3,9,1,512]{3,2,1,0:T(1,128)S(1)} %slice.256), channel_id=1, source_target_pairs={{0,1},{1,2},{2,3},{3,4},{4,5},{5,6},{6,7},{8,9},{9,10},{10,11},{11... | collective-permute-start | bytes 165896 | tf_op jit(solution)/shard_map/ppermute | solution.py:13
  277.1 8.4 %copy-start.13 = (f32[8,8,512]{2,1,0:T(8,128)S(1)}, f32[8,8,512]{2,1,0:T(8,128)}, u32[]{:S(2)}) copy-start(f32[8,8,512]{2,1,0:T(8,128)} %param.18) | copy-start | bytes 393220
  280.1 5.4 %collective-permute-start.3 = (f32[3,1,8,512]{3,2,1,0:T(8,128)S(1)}, f32[3,1,8,512]{3,2,1,0:T(8,128)S(1)}, u32[]{:S(2)}, u32[]{:S(2)}) collective-permute-start(f32[3,1,8,512]{3,2,1,0:T(8,128)S(1)} %slice.258), channel_id=1, source_target_pairs={{0,8},{8,16},{16,24},{1,9},{9,17},{17,25},{2,10},{10,18},{18,26},{... | collective-permute-start | bytes 147464 | tf_op jit(solution)/shard_map/ppermute | solution.py:13
  (6 other events, 5.0 us)
where the time goes:
time: 288 us; the launch traced here: 286 us
  other arithmetic  138 us (48%)
  local copies, waits for them, and re-layouts  117 us (41%)
  starting transfers between devices  22.2 us (8%)
  waiting for transfers between devices  8.67 us (3%)
    scatter-add x4, other arithmetic, per_device(): flat_forces = flat_forces.at[:, index].add(quarter)  98.5 us
    gather x7, local copies, waits for them, and re-layouts, per_device(): pieces.append(flat_disp[:, index] + shift_vec)  51.1 us
    scatter-add x1, other arithmetic, per_device(): jnp.zeros((3, slots), jnp.float32).at[:, flat_candidates]  13.1 us
    reshape x2, local copies, waits for them, and re-layouts, per_device(): flat_forces = forces.reshape(3, -1)  12.5 us
    scatter-add x1, local copies, waits for them, and re-layouts, per_device(): flat_forces = flat_forces.at[:, index].add(quarter)  12 us
    reshape x2, local copies, waits for them, and re-layouts, per_device(): flat_disp = extended[3:6].reshape(3, -1)  11.3 us
    ppermute x4, starting transfers between devices, shifted(): return lax.ppermute(array, axis, pairs)  10.6 us
    another operation x3, other arithmetic  9.41 us
  transfers between devices with their start and end apart: 6, of which 4 were waited for; matrix products, arithmetic and copies ran while one was open for 11% of the time, Pallas kernels for 0%

commit v1 on v0

--- a/solution.py
+++ b/solution.py
@@ -5,6 +5,13 @@
 
 time_step = 0.1
 penalty = 10.0
+
+
+def swap_blocks(x, mesh_axis, split, join):
+    size = lax.axis_size(mesh_axis)
+    blocks = jnp.stack(jnp.split(x, size, axis=split), axis=0)
+    blocks = lax.all_to_all(blocks, mesh_axis, split_axis=0, concat_axis=0)
+    return jnp.concatenate(blocks, axis=join)
 
 
 def shifted(array, axis, by):
@@ -142,13 +149,7 @@
     payload = jnp.concatenate([centre_own, area_own], 0)
     width = payload.shape[0]
     outgoing = jnp.zeros((width, slots), jnp.float32).at[:, target].set(payload)
-    arrived = lax.all_to_all(
-        outgoing.reshape(width, devices, capacity),
-        ("gx", "gy"),
-        split_axis=1,
-        concat_axis=1,
-        tiled=True,
-    )
+    arrived = swap_blocks(outgoing.reshape(width, devices, capacity), ("gx", "gy"), 1, 1)
     arrived = arrived.reshape(width, slots)
     centre = arrived[0:3]
     area = arrived[3:6]

time: 288 us -> 363 us (1.26)
  local copies, waits for them, and re-layouts: 117 us -> 192 us
    unnamed x58 -> x74, local copies, waits for them, and re-layouts: 5.55 us -> 53.5 us
    gather x7, local copies, waits for them, and re-layouts: 51.1 us -> 63.2 us  [per_device(): pieces.append(flat_disp[:, index] + shift_vec)]
    another operation x1 -> x3, local copies, waits for them, and re-layouts: 0.23 us -> 7.31 us  [the longest x2 7.08 us: swap_blocks(): blocks = jnp.stack(jnp.split(x, size, axis=split), axis=0)]
    split x0 -> x2, local copies, waits for them, and re-layouts: none -> 4.47 us  [swap_blocks(): blocks = jnp.stack(jnp.split(x, size, axis=split), axis=0)]
    another operation x4, other arithmetic: 5.17 us -> 1.34 us  [element_pass(): jnp.stack([-0.25 * (sign_x * tensor[row][0] + sign_y * tensor[row][1] + s...]
  transfers between devices with their start and end apart: 6 -> 6, of which waited for: 4 -> 4; matrix products, arithmetic and copies ran while one was open for 11% -> 9% of each run, Pallas kernels for 0% -> 0%
where the time goes in v1:
time: 363 us; the launch traced here: 360 us
  local copies, waits for them, and re-layouts  192 us (53%)
  other arithmetic  135 us (37%)
  starting transfers between devices  22.1 us (6%)
  waiting for transfers between devices  8.74 us (2%)
    scatter-add x4, other arithmetic, per_device(): flat_forces = flat_forces.at[:, index].add(quarter)  98.4 us
    gather x7, local copies, waits for them, and re-layouts, per_device(): pieces.append(flat_disp[:, index] + shift_vec)  63.2 us
    unnamed x74, local copies, waits for them, and re-layouts  53.5 us
    scatter-add x1, other arithmetic, per_device(): jnp.zeros((3, slots), jnp.float32).at[:, flat_candidates]  13.1 us
    reshape x2, local copies, waits for them, and re-layouts, per_device(): flat_disp = extended[3:6].reshape(3, -1)  12.5 us
    reshape x2, local copies, waits for them, and re-layouts, per_device(): flat_forces = forces.reshape(3, -1)  12.5 us
    scatter-add x1, local copies, waits for them, and re-layouts, per_device(): flat_forces = flat_forces.at[:, index].add(quarter)  12 us
    ppermute x4, starting transfers between devices, shifted(): return lax.ppermute(array, axis, pairs)  10.6 us
  transfers between devices with their start and end apart: 6, of which 4 were waited for; matrix products, arithmetic and copies ran while one was open for 9% of the time, Pallas kernels for 0%

profile of v1, /device:TPU:12, one launch (start us, length us, event | category | flops | bytes accessed | tf_op | source)
XLA Modules:
  0.0 359.6 jit_solution(2760515532182306431)
XLA Ops:
  4.8 9.1 %reduce-window.6 = s32[32,16,128]{2,1,0:T(8,128)S(1)} reduce-window(s32[32,16,128]{2,1,0:T(8,128)S(1)} %fusion.32, s32[]{:T(128)} %constant.89.clone.1), window={size=1x1x128 pad=0_0x0_0x127_0}, to_apply=%region_0.1 | reduce-window | flops 8323072 | bytes 524292 | tf_op jit(solution)/shard_map/reduce-window
  15.4 3.3 collective-permute-start.1
  19.6 3.2 collective-permute-done.1
  26.1 10.6 %copy.145 = f32[3,41553]{0,1:T(8,128)} copy(f32[3,41553]{1,0:T(4,128)S(1)} %reshape.125) | data formatting | bytes 997272 | tf_op jit(solution)/shard_map/reshape | solution.py:138
  36.7 14.6 %gather_fusion.3 = f32[2048,3]{1,0:T(8,128)} fusion(f32[3,41553]{0,1:T(8,128)} %copy.145, s32[2048]{0:T(1024)S(1)} %get-tuple-element.104), kind=kCustom, calls=%fused_computation.3 | custom fusion | bytes 57344 | tf_op jit(solution)/shard_map/gather | solution.py:146
  52.8 14.6 %gather_fusion.2 = f32[2048,3]{1,0:T(8,128)} fusion(f32[3,41553]{0,1:T(8,128)} %copy.145, s32[2048]{0:T(1024)S(1)} %get-tuple-element.102), kind=kCustom, calls=%fused_computation.2 | custom fusion | bytes 57344 | tf_op jit(solution)/shard_map/gather | solution.py:146
  71.3 14.6 %gather_fusion.1 = f32[2048,3]{1,0:T(8,128)} fusion(f32[3,41553]{0,1:T(8,128)} %copy.145, s32[2048]{0:T(1024)S(1)} %get-tuple-element.12), kind=kCustom, calls=%fused_computation.1 | custom fusion | bytes 57344 | tf_op jit(solution)/shard_map/gather | solution.py:146
  85.9 14.6 %gather_fusion = f32[2048,3]{1,0:T(8,128)} fusion(f32[3,41553]{0,1:T(8,128)} %copy.145, s32[2048]{0:T(1024)S(1)} %get-tuple-element.106), kind=kCustom, calls=%fused_computation | custom fusion | bytes 57344 | tf_op jit(solution)/shard_map/gather | solution.py:146
  105.3 7.4 %scatter_custom_fusion = f32[6,4096]{0,1:T(8,128)} fusion(s32[2048]{0:T(1024)S(1)} %bitcast.245, f32[2048,6]{1,0:T(8,128)} %copy.153, f32[]{:T(128)} %constant.80.clone.1), kind=kCustom, calls=%fused_computation.63 | custom fusion | bytes 98816 | tf_op jit(solution)/shard_map/scatter | solution.py:151
  167.9 5.4 %stack.294 = f32[32,6,1,128]{3,0,2,1:T(8,128)} concatenate(f32[1,6,1,128]{3,0,2,1:T(1,128)} %bitcast.263, f32[1,6,1,128]{3,0,2,1:T(1,128)} %bitcast.262, f32[1,6,1,128]{3,0,2,1:T(1,128)} %bitcast.261, f32[1,6,1,128]{3,0,2,1:T(1,128)} %bitcast.260, f32[1,6,1,128]{3,0,2,1:T(1,128)} %bitcast.259, f32[1,6,1,128]{3,0,2,1:T(1,128)} %bitcast.258, f32[1,6,1,128]{3,0,2,1:T(1,128)} %bitcast.257, ...), dimensions={0} | concatenate | bytes 196608 | tf_op jit(solution)/shard_map/stack | solution.py:12
  175.0 5.9 %all-to-all-start = ((f32[32,6,1,128]{3,2,1,0:T(1,128)}), f32[32,6,1,128]{3,2,1,0:T(1,128)}, u32[]{:S(2)}, u32[]{:S(2)}) async-start(f32[32,6,1,128]{3,2,1,0:T(1,128)} %copy.186), calls=%async_computation | async-start | bytes 196608 | tf_op jit(solution)/shard_map/all_to_all | solution.py:13
  180.9 4.6 %fusion = f32[3,9,9,513]{3,2,1,0:T(8,128)} fusion(f32[1,8,8,512]{3,2,1,0:T(8,128)S(1)} %get-tuple-element.85, f32[1,8,8,512]{3,2,1,0:T(8,128)S(1)} %get-tuple-element.79, f32[1,8,8,512]{3,2,1,0:T(8,128)S(1)} %get-tuple-element.72, f32[1,8,8,512]{3,2,1,0:T(8,128)S(1)} %get-tuple-element.84, f32[1,8,8,512]{3,2,1,0:T(8,128)S(1)} %get-tuple-element.78, ...), kind=kLoop, calls=%fused_computation.19 | loop fusion | flops 14086467 | bytes 3644364 | tf_op jit(solution)/shard_map/add | solution.py:74
  188.1 5.5 %gather_fusion.4 = f32[2048,6]{1,0:T(8,128)S(1)} fusion(f32[6,4096]{0,1:T(8,128)S(1)} %copy.189, s32[2048]{0:T(1024)S(1)} %get-tuple-element.108), kind=kCustom, calls=%fused_computation.4 | custom fusion | bytes 106496 | tf_op jit(solution)/shard_map/gather | solution.py:158
  195.9 13.1 %scatter_custom_fusion.1 = f32[3,4096]{0,1:T(8,128)S(1)} fusion(s32[2048]{0:T(1024)} %bitcast.249, f32[]{:T(128)} %constant.80.clone.1, f32[2048]{0:T(1024)S(1)} %maximum_multiply_fusion.1, f32[6,2048]{0,1:T(8,128)S(1)} %bitcast.229), kind=kCustom, calls=%fused_computation.58 | custom fusion | flops 18432 | bytes 107008 | tf_op jit(solution)/shard_map/scatter-add | solution.py:164
  210.3 5.6 %all-to-all-start.1 = ((f32[3,32,128]{2,0,1:T(4,128)}), f32[3,32,128]{2,0,1:T(4,128)S(1)}, u32[]{:S(2)}, u32[]{:S(2)}) async-start(f32[3,32,128]{2,0,1:T(4,128)} %copy.191), calls=%async_computation.1 | async-start | bytes 131072 | tf_op jit(solution)/shard_map/all_to_all | solution.py:165
  218.4 10.6 %copy.193 = f32[3,41553]{0,1:T(8,128)} copy(f32[3,41553]{1,0:T(4,128)S(1)} %reshape.122) | data formatting | bytes 997272 | tf_op jit(solution)/shard_map/reshape | solution.py:174
  229.7 5.5 %gather_fusion.5 = f32[2048,3]{1,0:T(8,128)S(1)} fusion(f32[3,4096]{0,1:T(8,128)S(1)} %bitcast.234, s32[2048]{0:T(1024)S(1)} %broadcast_clamp_fusion), kind=kCustom, calls=%fused_computation.5 | custom fusion | bytes 57344 | tf_op jit(solution)/shard_map/gather | solution.py:173
  235.2 24.6 %scatter_custom_fusion.2 = f32[3,41553]{0,1:T(8,128)} fusion(f32[3,41553]{0,1:T(8,128)} %copy.193, s32[2048]{0:T(1024)} %get-tuple-element.107, f32[2048,3]{1,0:T(8,128)S(1)} %gather_fusion.5, f32[]{:T(128)} %constant.81.clone.1), kind=kCustom, calls=%fused_computation.70 | custom fusion | flops 12288 | bytes 523724 | tf_op jit(solution)/shard_map/scatter-add | solution.py:176
  259.8 24.6 %scatter_custom_fusion.3 = f32[3,41553]{0,1:T(8,128)} fusion(f32[3,41553]{0,1:T(8,128)} %scatter_custom_fusion.2, s32[2048]{0:T(1024)} %get-tuple-element.13, f32[2048,3]{1,0:T(8,128)S(1)} %gather_fusion.5, f32[]{:T(128)} %constant.81.clone.1), kind=kCustom, calls=%fused_computation.68 | custom fusion | flops 12288 | bytes 523724 | tf_op jit(solution)/shard_map/scatter-add | solution.py:176
  284.4 24.6 %scatter_custom_fusion.4 = f32[3,41553]{0,1:T(8,128)} fusion(f32[3,41553]{0,1:T(8,128)} %scatter_custom_fusion.3, s32[2048]{0:T(1024)} %get-tuple-element.103, f32[2048,3]{1,0:T(8,128)S(1)} %gather_fusion.5, f32[]{:T(128)} %constant.81.clone.1), kind=kCustom, calls=%fused_computation.66 | custom fusion | flops 12288 | bytes 523724 | tf_op jit(solution)/shard_map/scatter-add | solution.py:176
  309.0 24.6 %scatter_custom_fusion.5 = f32[3,41553]{0,1:T(8,128)} fusion(f32[3,41553]{0,1:T(8,128)} %scatter_custom_fusion.4, s32[2048]{0:T(1024)} %get-tuple-element.105, f32[2048,3]{1,0:T(8,128)S(1)} %gather_fusion.5, f32[]{:T(128)} %constant.81.clone.1), kind=kCustom, calls=%fused_computation.72 | custom fusion | flops 12288 | bytes 523724 | tf_op jit(solution)/shard_map/scatter-add | solution.py:176
  333.6 12.0 %copy.194 = f32[3,41553]{1,0:T(4,128)S(1)} copy(f32[3,41553]{0,1:T(8,128)} %scatter_custom_fusion.5) | data formatting | bytes 997272 | tf_op jit(solution)/shard_map/scatter-add | solution.py:176
  346.2 3.5 collective-permute-start.2
  350.4 2.9 collective-permute-done.2
  (133 shorter events, 93.4 us)
Async XLA Ops:
  0.6 4.0 %copy-start.10 = (s32[4,512]{1,0:T(4,128)S(1)}, s32[4,512]{1,0:T(4,128)}, u32[]{:S(2)}) copy-start(s32[4,512]{1,0:T(4,128)} %param.23) | copy-start | bytes 24580
  0.6 4.1 %copy-start.7 = (s32[2048,1]{0,1:T(1,128)S(1)}, s32[2048,1]{0,1:T(1,128)}, u32[]{:S(2)}) copy-start(s32[2048,1]{0,1:T(1,128)} %param.21) | copy-start | bytes 24580
  2.7 12.7 %collective-permute-start = (f32[6,1,8,512]{3,2,1,0:T(8,128)S(1)}, f32[6,1,8,512]{3,2,1,0:T(8,128)S(1)}, u32[]{:S(2)}, u32[]{:S(2)}) collective-permute-start(f32[6,1,8,512]{3,2,1,0:T(8,128)S(1)} %slice.231), channel_id=1, source_target_pairs={{8,0},{16,8},{24,16},{9,1},{17,9},{25,17},{10,2},{18,10},{26,18},{... | collective-permute-start | bytes 294920 | tf_op jit(solution)/shard_map/ppermute | solution.py:20
  4.7 10.0 %copy-start.8 = (s32[2048,1]{0,1:T(1,128)}, s32[2048,1]{0,1:T(1,128)S(1)}, u32[]{:S(2)}) copy-start(s32[2048,1]{0,1:T(1,128)S(1)} %compare_select_fusion.1) | copy-start | bytes 24580
  4.8 10.0 %copy-start.11 = (s32[2048]{0:T(1024)S(1)}, s32[2048]{0:T(1024)}, u32[]{:S(2)}) copy-start(s32[2048]{0:T(1024)} %param.20) | copy-start | bytes 24580
  14.0 4.8 %copy-start.9 = (f32[3,512]{1,0:T(4,128)S(1)}, f32[3,512]{1,0:T(4,128)}, u32[]{:S(2)}) copy-start(f32[3,512]{1,0:T(4,128)} %param.22) | copy-start | bytes 18436
  15.4 7.4 %collective-permute-start.1 = (f32[6,9,1,512]{3,2,1,0:T(1,128)S(1)}, f32[6,9,1,512]{3,2,1,0:T(1,128)S(1)}, u32[]{:S(2)}, u32[]{:S(2)}) collective-permute-start(f32[6,9,1,512]{3,2,1,0:T(1,128)S(1)} %pad_maximum_fusion.3), channel_id=1, source_target_pairs={{1,0},{2,1},{3,2},{4,3},{5,4},{6,5},{7,6},{9,8},{10,9},{11,10},{12... | collective-permute-start | bytes 331784 | tf_op jit(solution)/shard_map/ppermute | solution.py:20
  100.5 3.2 copy-start.12
  100.5 3.2 copy-start.13
  100.5 3.2 copy-start.14
  114.7 2.4 copy-start.1
  117.6 1.0 copy-start.2
  117.6 1.2 copy-start.3
  117.7 1.2 copy-start.5
  122.2 45.0 %copy-start.4 = (f32[6,1,128]{0,2,1:T(8,128)S(1)}, f32[6,1,128]{0,2,1:T(8,128)}, u32[]{:S(2)}) copy-start(f32[6,1,128]{0,2,1:T(8,128)} %get-tuple-element.51) | copy-start | bytes 9220
  175.0 11.5 %all-to-all-start = ((f32[32,6,1,128]{3,2,1,0:T(1,128)}), f32[32,6,1,128]{3,2,1,0:T(1,128)}, u32[]{:S(2)}, u32[]{:S(2)}) async-start(f32[32,6,1,128]{3,2,1,0:T(1,128)} %copy.186), calls=%async_computation | async-start | bytes 196608 | tf_op jit(solution)/shard_map/all_to_all | solution.py:13
  210.3 18.8 %all-to-all-start.1 = ((f32[3,32,128]{2,0,1:T(4,128)}), f32[3,32,128]{2,0,1:T(4,128)S(1)}, u32[]{:S(2)}, u32[]{:S(2)}) async-start(f32[3,32,128]{2,0,1:T(4,128)} %copy.191), calls=%async_computation.1 | async-start | bytes 131072 | tf_op jit(solution)/shard_map/all_to_all | solution.py:165
  346.2 9.1 %copy-start = (f32[3,2048]{0,1:T(8,128)S(1)}, f32[3,2048]{0,1:T(8,128)}, u32[]{:S(2)}) copy-start(f32[3,2048]{0,1:T(8,128)} %get-tuple-element.66) | copy-start | bytes 73732
  346.2 7.1 %collective-permute-start.2 = (f32[3,9,1,512]{3,2,1,0:T(1,128)S(1)}, f32[3,9,1,512]{3,2,1,0:T(1,128)S(1)}, u32[]{:S(2)}, u32[]{:S(2)}) collective-permute-start(f32[3,9,1,512]{3,2,1,0:T(1,128)S(1)} %slice.256), channel_id=1, source_target_pairs={{0,1},{1,2},{2,3},{3,4},{4,5},{5,6},{6,7},{8,9},{9,10},{10,11},{11... | collective-permute-start | bytes 165896 | tf_op jit(solution)/shard_map/ppermute | solution.py:20
  350.4 8.4 %copy-start.6 = (f32[8,8,512]{2,1,0:T(8,128)S(1)}, f32[8,8,512]{2,1,0:T(8,128)}, u32[]{:S(2)}) copy-start(f32[8,8,512]{2,1,0:T(8,128)} %param.18) | copy-start | bytes 393220
  353.4 5.4 %collective-permute-start.3 = (f32[3,1,8,512]{3,2,1,0:T(8,128)S(1)}, f32[3,1,8,512]{3,2,1,0:T(8,128)S(1)}, u32[]{:S(2)}, u32[]{:S(2)}) collective-permute-start(f32[3,1,8,512]{3,2,1,0:T(8,128)S(1)} %slice.258), channel_id=1, source_target_pairs={{0,8},{8,16},{16,24},{1,9},{9,17},{17,25},{2,10},{10,18},{18,26},{... | collective-permute-start | bytes 147464 | tf_op jit(solution)/shard_map/ppermute | solution.py:20
